TPU v7x, 32 devices: a whole 2x2x4 slice. The times are simulated.
32 devices in a mesh: rows: 8 (over z, y), grp: 4 (over x, core).
Axes of the slice: x: 2, y: 2, z: 4, core: 2. Of those that a mesh axis runs over, the one named last changes fastest.
Arguments:
- features: bfloat16 [192, 128, 2048], P('rows', None, 'grp'), may hold values from 0 to 12
- depth_weight: float32 [3, 3, 3, 2048], P(None, None, None, 'grp'), may hold values from -2 to 2
- branch_weight: bfloat16 [4, 2048, 256], P(None, 'grp'), may hold values from -0.125 to 0.125
- pool_weight: bfloat16 [2048, 256], P('grp'), may hold values from -0.125 to 0.125
- proj_weight: bfloat16 [5, 256, 256], P(None, 'grp'), may hold values from -0.15625 to 0.15625
- class_weight: bfloat16 [256, 11], replicated, may hold values from -0.375 to 0.375
- labels: int32 [192, 128], P('rows'), may hold values from 0 to 11
Outputs:
- grad_branch: float32 [4, 2048, 256], P(None, 'grp')
- grad_depth: float32 [3, 3, 3, 2048], P(None, None, None, 'grp')
- grad_pool: float32 [2048, 256], P('grp')
- grad_proj: float32 [5, 256, 256], P(None, 'grp')
- grad_class: float32 [256, 11], replicated
All inputs are finite; a program needn't handle non-finite values.
Results may differ from a plain program's by a relative error of at most 0.0056.
Values may be sent and summed in bfloat16 or wider, within the bound.
A program may use at most 128 MiB of HBM per device.

v0:
```python
import math
import jax
import jax.numpy as jnp
from jax import lax
from jax.sharding import PartitionSpec as P

RATES = (6, 12, 18)
MARGIN = 18


def padded_2(block, sides, width):
    for axis, dim in sides:
        count = lax.axis_size(axis)
        forward = [(i, i + 1) for i in range(count - 1)]
        backward = [(target, source) for source, target in forward]
        low = lax.ppermute(
            lax.slice_in_dim(block, block.shape[dim] - width, None, axis=dim), axis, forward
        )
        high = lax.ppermute(lax.slice_in_dim(block, 0, width, axis=dim), axis, backward)
        block = jnp.concatenate([low, block, high], axis=dim)
    return block


def depth_taps(padded, weights, height, width):
    outputs = []
    for index, rate in enumerate(RATES):
        total = jnp.zeros((height, width, padded.shape[2]), jnp.float32)
        for row_tap in range(3):
            for col_tap in range(3):
                row_start = MARGIN + (row_tap - 1) * rate
                col_start = MARGIN + (col_tap - 1) * rate
                total = (
                    total
                    + weights[index, row_tap, col_tap]
                    * padded[row_start : row_start + height, col_start : col_start + width]
                )
        outputs.append(total.astype(jnp.bfloat16))
    return outputs


def depth_grads(padded, backs, height, width):
    result = []
    for index, rate in enumerate(RATES):
        taps = []
        for row_tap in range(3):
            for col_tap in range(3):
                row_start = MARGIN + (row_tap - 1) * rate
                col_start = MARGIN + (col_tap - 1) * rate
                window = padded[row_start : row_start + height, col_start : col_start + width]
                taps.append(jnp.sum(backs[index] * window, axis=(0, 1)))
        result.append(jnp.stack(taps).reshape(3, 3, -1))
    return jnp.stack(result)


def class_head(mixed, class_weight, labels, total_pixels):
    f32 = jnp.float32
    classes = class_weight.shape[1]
    hidden = jnp.maximum(mixed, 0.0).astype(jnp.bfloat16)
    logits = jnp.einsum("pc,ck->kp", hidden, class_weight, preferred_element_type=f32)
    expo = jnp.exp(logits)
    soft = expo / jnp.sum(expo, axis=0, keepdims=True)
    label_row = labels.reshape(-1)
    onehot = (
        lax.broadcasted_iota(jnp.int32, (classes, label_row.shape[0]), 0) == label_row[None, :]
    ).astype(f32)
    valid = (label_row < classes).astype(f32)
    grad_logit = ((soft - onehot) * valid[None, :] / math.sqrt(total_pixels)).astype(jnp.bfloat16)
    class_part = jnp.einsum("pc,kp->ck", hidden, grad_logit, preferred_element_type=f32)
    back_hidden = jnp.einsum("ck,kp->pc", class_weight, grad_logit, preferred_element_type=f32)
    grad_mixed = (back_hidden * (mixed > 0)).astype(jnp.bfloat16)
    col_total = lax.psum(jnp.sum(grad_mixed.astype(f32), axis=0), "rows")
    return (grad_mixed, col_total, class_part)


def per_device(
    features, depth_weight, branch_weight, pool_weight, proj_weight, class_weight, labels
):
    f32 = jnp.float32
    highest = lax.Precision.HIGHEST
    height, width, local_in = features.shape
    pixels_local = height * width
    total_pixels = height * lax.axis_size("rows") * width
    halo_rows = padded_2(features, (("rows", 0),), MARGIN)
    padded = jnp.pad(halo_rows.astype(f32), ((0, 0), (MARGIN, MARGIN), (0, 0)))
    depth_out = depth_taps(padded, depth_weight, height, width)
    flat_inputs = [item.reshape(pixels_local, local_in) for item in [features] + depth_out]
    column_sum = jnp.sum(features.astype(f32), axis=(0, 1))
    pooled = lax.psum(column_sum, "rows") / total_pixels
    partial_pre = jnp.stack(
        [jnp.dot(flat_inputs[k], branch_weight[k], preferred_element_type=f32) for k in range(4)]
    )
    pool_part = jnp.dot(pooled, pool_weight.astype(f32), precision=highest)[None, None, :]
    pre, pool_pre = (
        lax.psum_scatter(partial_pre, "grp", scatter_dimension=2, tiled=True),
        lax.psum_scatter(pool_part, "grp", scatter_dimension=2, tiled=True),
    )
    pool_pre = pool_pre[0, 0]
    own_out = jnp.maximum(pre, 0.0).astype(jnp.bfloat16)
    own_pool = jnp.maximum(pool_pre, 0.0).astype(jnp.bfloat16)
    mixed_part = jnp.einsum("kpc,kcd->pd", own_out, proj_weight[:4], preferred_element_type=f32)
    mixed_part = (
        mixed_part
        + jnp.dot(own_pool.astype(f32), proj_weight[4].astype(f32), precision=highest)[None, :]
    )
    mixed = lax.psum(mixed_part, "grp")
    grad_mixed, col_total, class_part = class_head(mixed, class_weight, labels, total_pixels)
    back_pre = jnp.einsum("pd,kcd->kpc", grad_mixed, proj_weight[:4], preferred_element_type=f32)
    own_grad = (back_pre * (pre > 0)).astype(jnp.bfloat16)
    own_poolgrad = (
        jnp.dot(col_total, proj_weight[4].astype(f32).T, precision=highest) * (pool_pre > 0)
    ).astype(jnp.bfloat16)
    grad_pre, grad_poolpre = (
        lax.all_gather(own_grad, "grp", axis=2, tiled=True),
        lax.all_gather(own_poolgrad[None, None, :], "grp", axis=2, tiled=True),
    )
    grad_poolpre = grad_poolpre[0, 0]
    proj_part = jnp.einsum("kpc,pd->kcd", own_out, grad_mixed, preferred_element_type=f32)
    pool_proj = own_pool.astype(f32)[:, None] * col_total[None, :]
    branch_part = jnp.stack(
        [
            jnp.einsum("pc,pd->cd", flat_inputs[k], grad_pre[k], preferred_element_type=f32)
            for k in range(4)
        ]
    )
    backs = [
        jnp.einsum(
            "pd,cd->pc", grad_pre[k + 1], branch_weight[k + 1], preferred_element_type=f32
        ).reshape(height, width, local_in)
        for k in range(3)
    ]
    depth_part = depth_grads(padded, backs, height, width)
    grad_pool = pooled[:, None] * grad_poolpre.astype(f32)[None, :]
    grad_branch, grad_depth, proj_main, grad_class = lax.psum(
        (branch_part, depth_part, proj_part, class_part), "rows"
    )
    grad_proj = jnp.concatenate([proj_main, pool_proj[None]], axis=0)
    return (grad_branch, grad_depth, grad_pool, grad_proj, grad_class)


def solution(mesh):
    return jax.shard_map(
        per_device,
        mesh=mesh,
        in_specs=(
            P("rows", None, "grp"),
            P(None, None, None, "grp"),
            P(None, "grp", None),
            P("grp", None),
            P(None, "grp", None),
            P(),
            P("rows", None),
        ),
        out_specs=(
            P(None, "grp", None),
            P(None, None, None, "grp"),
            P("grp", None),
            P(None, "grp", None),
            P(),
        ),
        check_vma=False,
    )
```

profile of v0, /device:TPU:0, one launch (start us, length us, event | category | flops | bytes accessed | tf_op | source)
XLA Modules:
  0.0 927.9 jit_solution(12588569372178841400)
XLA Ops:
  7.2 5.2 fusion.69
  12.4 6.3 collective-permute-start
  18.7 1.3 collective-permute-start.1
  20.0 0.5 convert_reduce_fusion
  20.4 110.5 %psum.49 = f32[512]{0:T(512)S(1)} all-reduce(f32[512]{0:T(512)S(1)} %convert_reduce_fusion), channel_id=1, replica_groups=mesh['rows'=8,'grp'=4] {'rows'}, use_global_device_ids=true, to_apply=%region_2.3 | all-reduce | flops 512 | bytes 4096 | tf_op jit(solution)/shard_map/psum | solution.py:88
  131.0 1.1 convolution_bitcast_fusion.6
  132.2 1.9 convolution_bitcast_fusion.5
  134.2 8.1 maximum_convert_fusion
  142.3 24.1 %add_convert_fusion.1 = bf16[24,128,512]{2,1,0:T(8,128)(2,1)S(1)} fusion(f32[60,128,512]{2,1,0:T(8,128)} %maximum_convert_fusion, f32[512]{0:T(512)S(1)} %bitcast.242, f32[512]{0:T(512)S(1)} %bitcast.243, f32[512]{0:T(512)S(1)} %bitcast.244, f32[512]{0:T(512)S(1)} %bitcast.245, f32[512]{0:T(512)S(1)} %bitcast.246, f32[512]{0:T(512)S(1)} %bitcast.247, ...), kind=kLoop, calls=%fused_computation.49 | loop fusion | flops 28311552 | bytes 37767168 | tf_op jit(solution)/shard_map/convert_element_type | solution.py:37
  166.3 2.1 convolution_bitcast_fusion.3
  168.5 19.2 %add_convert_fusion = bf16[24,128,512]{2,1,0:T(8,128)(2,1)S(1)} fusion(f32[60,128,512]{2,1,0:T(8,128)} %maximum_convert_fusion, f32[512]{0:T(512)S(1)} %bitcast.230, f32[512]{0:T(512)S(1)} %bitcast.231, f32[512]{0:T(512)S(1)} %bitcast.235, f32[512]{0:T(512)S(1)} %bitcast.236, f32[512]{0:T(512)S(1)} %bitcast.237, f32[512]{0:T(512)S(1)} %bitcast.238, ...), kind=kLoop, calls=%fused_computation.48 | loop fusion | flops 28311552 | bytes 37767168 | tf_op jit(solution)/shard_map/convert_element_type | solution.py:37
  187.7 1.7 copy-done.3
  189.4 3.6 convolution_bitcast_fusion.2
  193.0 24.6 %add_convert_fusion.2 = bf16[24,128,512]{2,1,0:T(8,128)(2,1)S(1)} fusion(f32[60,128,512]{2,1,0:T(8,128)} %maximum_convert_fusion, f32[512]{0:T(512)S(1)} %bitcast.233, f32[512]{0:T(512)S(1)} %bitcast.234, f32[512]{0:T(512)S(1)} %bitcast.225, f32[512]{0:T(512)S(1)} %bitcast.226, f32[512]{0:T(512)S(1)} %bitcast.227, f32[512]{0:T(512)S(1)} %bitcast.228, ...), kind=kLoop, calls=%fused_computation.50 | loop fusion | flops 28311552 | bytes 37767168 | tf_op jit(solution)/shard_map/convert_element_type | solution.py:37
  217.6 1.6 copy-done.5
  219.2 2.4 convolution_bitcast_fusion.4
  221.6 4.9 pad_maximum_fusion
  226.5 15.3 %copy.30 = f32[4,3072,256]{1,0,2:T(4,128)} copy(f32[4,3072,256]{2,1,0:T(8,128)} %pad_maximum_fusion) | data formatting | bytes 25165824 | tf_op jit(solution)/shard_map/stack | solution.py:89
  241.9 0.6 all-reduce.10.cloned.1.call-start
  242.5 0.0 copy-done.16
  242.5 0.6 fusion.72
  243.8 0.8 copy.46
  244.7 0.1 fusion.53
  244.8 217.1 %all-reduce.12.cloned.1.call-done = f32[4,3072,256]{1,0,2:T(4,128)} async-done(((f32[4,3072,256]{1,0,2:T(4,128)}), f32[4,3072,256]{1,0,2:T(4,128)}) %all-reduce.12.cloned.1.call-update) | async-done | bytes 12582928
  461.9 2.1 constant_dynamic-slice_fusion
  464.0 1.6 copy-done.7
  465.6 3.8 fusion.1
  469.5 68.7 %all-reduce.10.cloned.1.call-done = f32[3072,256]{1,0:T(8,128)} async-done(((f32[3072,256]{1,0:T(8,128)}), f32[3072,256]{1,0:T(8,128)}) %all-reduce.10.cloned.1.call-update) | async-done | bytes 3145744 | tf_op jit(solution)/shard_map/psum | solution.py:105
  538.2 2.6 fusion.73
  540.8 3.2 convert_reduce_fusion.1
  544.1 3.3 fusion.3
  547.4 2.4 copy.33
  549.8 0.0 all-reduce.14.cloned.1.call-start
  549.8 2.8 fusion.29
  552.7 5.0 fusion.12
  557.7 38.8 %all-gather.3.cloned.1.call-done = bf16[4,3072,256]{1,0,2:T(4,128)(2,1)} async-done(((bf16[4,3072,64]{1,0,2:T(4,128)(2,1)}), bf16[4,3072,256]{1,0,2:T(4,128)(2,1)}) %all-gather.3.cloned.1.call-update) | async-done | bytes 6291472 | tf_op jit(solution)/shard_map/all_gather | solution.py:113
  596.4 18.7 %fusion.68 = (bf16[1,3072,256]{1,0,2:T(2,128)(2,1)}, bf16[1,3072,256]{1,0,2:T(2,128)(2,1)}, bf16[1,3072,256]{1,0,2:T(2,128)(2,1)}, bf16[1,3072,256]{1,0,2:T(2,128)(2,1)}) fusion(bf16[4,3072,256]{1,0,2:T(4,128)(2,1)} %all-gather.3.cloned.1.call-done), kind=kLoop, calls=%fused_computation.133 | loop fusion | bytes 12582912 | tf_op jit(solution)/shard_map/slice | solution.py:121
  615.2 7.3 copy.48
  622.5 4.3 fusion.18
  626.8 24.8 %multiply_reduce_fusion.18 = (f32[512]{0:T(512)S(1)}, f32[512]{0:T(512)S(1)}, f32[512]{0:T(512)S(1)}, f32[512]{0:T(512)S(1)}, f32[512]{0:T(512)S(1)}, /*index=5*...) fusion(f32[60,128,512]{2,1,0:T(8,128)} %maximum_convert_fusion, ...), kind=kOutput, calls=%fused_computation.38 | convolution fusion | flops 833613312 | bytes 36456448 | tf_op jit(solution)/shard_map/pd,cd->pc/dot_general | solution.py:126
  651.5 0.1 stack.142
  651.6 7.3 copy.49
  658.9 4.3 fusion.21
  663.2 24.1 %multiply_reduce_fusion.9 = (f32[512]{0:T(512)S(1)}, f32[512]{0:T(512)S(1)}, f32[512]{0:T(512)S(1)}, f32[512]{0:T(512)S(1)}, f32[512]{0:T(512)S(1)}, /*index=5*/...) fusion(f32[60,128,512]{2,1,0:T(8,128)} %maximum_convert_fusion, ...), kind=kOutput, calls=%fused_computation.29 | convolution fusion | flops 833613312 | bytes 36456448 | tf_op jit(solution)/shard_map/pd,cd->pc/dot_general | solution.py:126
  687.3 0.1 stack.152
  687.4 7.3 copy.50
  694.7 4.2 fusion.24
  698.9 20.2 %multiply_reduce_fusion = (f32[512]{0:T(512)S(1)}, f32[512]{0:T(512)S(1)}, f32[512]{0:T(512)S(1)}, f32[512]{0:T(512)S(1)}, f32[512]{0:T(512)S(1)}, /*index=5*/f3...) fusion(f32[60,128,512]{2,1,0:T(8,128)} %maximum_convert_fusion, bf16[24,128,256]{2,1,0:T(8,128)(2,1)} %bitcast.217, ...), kind=kOutput, calls=%fused_computation.20 | convolution fusion | flops 833613312 | bytes 36456448 | tf_op jit(solution)/shard_map/pd,cd->pc/dot_general | solution.py:126
  719.1 0.1 stack.162
  719.2 7.3 copy.47
  726.5 3.2 fusion.15
  729.7 0.6 pad_maximum_fusion.3
  730.5 3.0 pad_maximum_fusion.1
  734.1 66.5 %all-reduce.14.cloned.1.call-done = (f32[3,3,3,512]{3,2,1,0:T(4,128)}, f32[256]{0:T(256)}, f32[256,11]{0,1:T(8,128)}) async-done(((f32[3,3,3,512]{3,2,1,0:T(4,128)}, f32[256]{0:T(256)}, f32[256,11]{0,1:T(8,128)}), (f32[3,3,3,512]{3,2,1,0:T(4,128)}, f32[256]{0:T(256)}, f32[256,11]{0,1:T(8,128)})) %all-reduce.14.cloned.1.call-update) | async-done | bytes 67600 | tf_op jit(solution)/shard_map/psum | solution.py:133
  800.7 0.9 fusion.28
  801.5 0.3 dynamic-update-slice
  801.8 5.6 all-reduce.1
  807.4 0.7 broadcast_multiply_fusion.1
  808.2 0.9 broadcast_multiply_fusion
  809.1 104.3 %all-reduce.16.cloned.1.call-done = (f32[4,512,256]{1,2,0:T(8,128)}, f32[4,64,256]{2,1,0:T(8,128)}) async-done(((f32[4,512,256]{1,2,0:T(8,128)}, f32[4,64,256]{2,1,0:T(8,128)}), (f32[4,512,256]{1,2,0:T(8,128)}, f32[4,64,256]{2,1,0:T(8,128)})) %all-reduce.16.cloned.1.call-update) | async-done | bytes 2359312 | tf_op jit(solution)/shard_map/psum | solution.py:133
  913.4 2.9 copy.41
  916.3 1.7 pad_maximum_fusion.2
  918.0 1.5 copy.63
  919.5 1.3 copy.64
  (53 shorter events, 0.5 us)
Async XLA Ops:
  7.2 123.8 %copy-start = (bf16[512,256]{1,0:T(8,128)(2,1)S(1)}, bf16[512,256]{1,0:T(8,128)(2,1)}, u32[]{:S(2)}) copy-start(bf16[512,256]{1,0:T(8,128)(2,1)} %param.10) | copy-start | bytes 786436
  7.2 12.8 %copy-start.2 = (bf16[24,128,512]{2,1,0:T(8,128)(2,1)S(1)}, bf16[24,128,512]{2,1,0:T(8,128)(2,1)}, u32[]{:S(2)}) copy-start(bf16[24,128,512]{2,1,0:T(8,128)(2,1)} %param.7) | copy-start | bytes 9437188
  7.2 125.0 %copy-start.13 = (f32[3,3,3,512]{3,2,1,0:T(4,128)S(1)}, f32[3,3,3,512]{3,2,1,0:T(4,128)}, u32[]{:S(2)}) copy-start(f32[3,3,3,512]{3,2,1,0:T(4,128)} %param.8) | copy-start | bytes 165892
  7.2 236.6 %reduce-scatter.4.cloned.1.call-start = ((), (), s32[]{:S(2)}) async-start(), calls=%async_computation.3 | async-start | bytes 163840
  12.4 121.8 %collective-permute-start = (bf16[18,128,512]{2,1,0:T(8,128)(2,1)}, bf16[18,128,512]{2,1,0:T(8,128)(2,1)}, u32[]{:S(2)}, u32[]{:S(2)}) collective-permute-start(bf16[18,128,512]{2,1,0:T(8,128)(2,1)} %get-tuple-element.56), channel_id=1, source_target_pairs={{0,4},{4,8},{8,12},{12,16},{16,20},{20,24},{24,28},{1,5},{5,9},{9,... | collective-permute-start | bytes 7077896 | tf_op jit(solution)/shard_map/ppermute | solution.py:16
  18.7 115.5 %collective-permute-start.1 = (bf16[18,128,512]{2,1,0:T(8,128)(2,1)}, bf16[18,128,512]{2,1,0:T(8,128)(2,1)}, u32[]{:S(2)}, u32[]{:S(2)}) collective-permute-start(bf16[18,128,512]{2,1,0:T(8,128)(2,1)} %get-tuple-element.57), channel_id=1, source_target_pairs={{4,0},{8,4},{12,8},{16,12},{20,16},{24,20},{28,24},{5,1},{9,5},{13... | collective-permute-start | bytes 7077896 | tf_op jit(solution)/shard_map/ppermute | solution.py:19
  132.1 329.7 %all-reduce.12.cloned.1.call-start = ((), (), s32[]{:S(2)}) async-start(), calls=%async_computation.4 | async-start | bytes 25165824
  166.3 2.1 copy-start.4
  187.7 1.7 copy-start.3
  217.6 1.6 copy-start.5
  217.6 4.0 copy-start.6
  241.8 0.7 copy-start.16
  241.8 2.8 copy-start.15
  241.9 296.4 %all-reduce.10.cloned.1.call-start = ((), (), s32[]{:S(2)}) async-start(), calls=%async_computation.1 | async-start | bytes 6291456 | tf_op jit(solution)/shard_map/psum | solution.py:105
  464.0 1.7 copy-start.7
  464.0 5.5 copy-start.12
  464.0 74.3 %copy-start.14 = (bf16[256,11]{0,1:T(8,128)(2,1)S(1)}, bf16[256,11]{0,1:T(8,128)(2,1)}, u32[]{:S(2)}) copy-start(bf16[256,11]{0,1:T(8,128)(2,1)} %param.12) | copy-start | bytes 16900
  469.4 127.0 %all-gather.3.cloned.1.call-start = ((), (), s32[]{:S(2)}) async-start(), calls=%async_computation.2 | async-start | bytes 7864320 | tf_op jit(solution)/shard_map/all_gather | solution.py:113
  538.2 5.8 copy-start.8
  544.1 3.3 copy-start.9
  549.8 250.9 %all-reduce.14.cloned.1.call-start = ((), (), s32[]{:S(2)}) async-start(), calls=%async_computation.5 | async-start | bytes 182272 | tf_op jit(solution)/shard_map/psum | solution.py:133
  622.5 4.3 copy-start.10
  658.9 4.3 copy-start.11
  726.5 194.3 %copy-start.1 = (bf16[512,256]{1,0:T(8,128)(2,1)S(1)}, bf16[512,256]{1,0:T(8,128)(2,1)}, u32[]{:S(2)}) copy-start(bf16[512,256]{1,0:T(8,128)(2,1)} %param.10) | copy-start | bytes 786436
  730.4 183.0 %all-reduce.16.cloned.1.call-start = ((), (), s32[]{:S(2)}) async-start(), calls=%async_computation.6 | async-start | bytes 4718592 | tf_op jit(solution)/shard_map/psum | solution.py:133
Sparse Core Ops, SparseCore 0:
  132.2 18.7 reduce-scatter.3
  242.0 219.8 all-reduce.11
  469.5 68.6 all-reduce.9
  549.9 46.4 all-gather.2
  730.5 70.0 all-reduce.13
  805.1 108.2 all-reduce.15
where the time goes:
time: 932 us; the launch traced here: 928 us
  waiting for transfers between devices  496 us (53%)
  matrix products  118 us (13%)
  blocking collectives  116 us (12%)
  other arithmetic  88.4 us (9%)
  local copies, waits for them, and re-layouts  85.7 us (9%)
  between operations  15.9 us (2%)
    unnamed x8, waiting for transfers between devices  217 us
    psum x2, waiting for transfers between devices, per_device(): lax.psum((branch_part, depth_part, proj_part, class_part), 'rows')  171 us
    psum x1, blocking collectives, per_device(): pooled = lax.psum(column_sum, 'rows') / total_pixels  111 us
    dot_general x3, matrix products, per_device(): jnp.einsum('pd,cd->pc', grad_pre[k + 1], branch_weight[k + 1], preferred_...  69 us
    psum x1, waiting for transfers between devices, per_device(): mixed = lax.psum(mixed_part, 'grp')  68.7 us
    convert_element_type x3, other arithmetic, depth_taps(): outputs.append(total.astype(jnp.bfloat16))  67.9 us
    unnamed x46, local copies, waits for them, and re-layouts  43.9 us
    all_gather x1, waiting for transfers between devices, per_device(): lax.all_gather(own_grad, 'grp', axis=2, tiled=True)  38.8 us
  transfers between devices with their start and end apart: 8, of which 5 were waited for; matrix products, arithmetic and copies ran while one was open for 13% of the time, Pallas kernels for 0%

commit v1 on v0

--- a/solution.py
+++ b/solution.py
@@ -109,8 +109,35 @@
     own_poolgrad = (
         jnp.dot(col_total, proj_weight[4].astype(f32).T, precision=highest) * (pool_pre > 0)
     ).astype(jnp.bfloat16)
+
+    def _supply_view(group_axis, buf):
+        f_next = lax.axis_size(group_axis)
+        local_part = lax.axis_index(group_axis)
+        res, row_out, right_arr = (f_next, local_part, buf.shape[2])
+        piece_out = range(res)
+        last = map(lambda it: (it, (it + 1) % res), piece_out)
+        shelf = list(last)
+        r_now = range(res)
+        raw_out = map(lambda it: (it, (it - 1) % res), r_now)
+        rack = list(raw_out)
+        frame_out = jnp.zeros((*buf.shape[:2], res * right_arr, *buf.shape[3:]), buf.dtype)
+        frame_out = lax.dynamic_update_slice_in_dim(frame_out, buf, row_out * right_arr, axis=2)
+        lower = kept_arr = buf
+        wide_out = res // 2
+        for dev in [*range(1, wide_out + 1)]:
+            lower = lax.ppermute(lower, group_axis, shelf)
+            frame_out = lax.dynamic_update_slice_in_dim(
+                frame_out, lower, (row_out - dev) % res * right_arr, axis=2
+            )
+            if dev < res - wide_out:
+                kept_arr = lax.ppermute(kept_arr, group_axis, rack)
+                frame_out = lax.dynamic_update_slice_in_dim(
+                    frame_out, kept_arr, (row_out + dev) % res * right_arr, axis=2
+                )
+        return frame_out
+
     grad_pre, grad_poolpre = (
-        lax.all_gather(own_grad, "grp", axis=2, tiled=True),
+        _supply_view("grp", own_grad),
         lax.all_gather(own_poolgrad[None, None, :], "grp", axis=2, tiled=True),
     )
     grad_poolpre = grad_poolpre[0, 0]

time: 932 us -> 1030 us (1.11)
  local copies, waits for them, and re-layouts: 85.7 us -> 186 us
  waiting for transfers between devices: 496 us -> 481 us
  starting transfers between devices: 8.31 us -> 21.5 us
    dynamic_update_slice x0 -> x4, local copies, waits for them, and re-layouts: none -> 128 us  [the longest x2 62.9 us: _supply_view(): lax.dynamic_update_slice_in_dim(frame_out, lower, (row_out - dev) % res *...]
    all_gather x1 -> x0, waiting for transfers between devices: 38.8 us -> none  [per_device(): lax.all_gather(own_grad, 'grp', axis=2, tiled=True)]
    ppermute x0 -> x3, waiting for transfers between devices: none -> 34.6 us  [the longest x2 34.6 us: _supply_view(): lower = lax.ppermute(lower, group_axis, shelf)]
    unnamed x46 -> x56, local copies, waits for them, and re-layouts: 43.9 us -> 13.6 us
    slice x1, local copies, waits for them, and re-layouts: 18.7 us -> 4.53 us  [per_device(): grad_pre[k]]
    ppermute x0 -> x3, local copies, waits for them, and re-layouts: none -> 12.5 us  [the longest x2 8.31 us: _supply_view(): lower = lax.ppermute(lower, group_axis, shelf)]
    unnamed x8 -> x7, waiting for transfers between devices: 217 us -> 206 us
    psum x1, starting transfers between devices: 0.57 us -> 12.1 us  [per_device(): mixed = lax.psum(mixed_part, 'grp')]
  transfers between devices with their start and end apart: 8 -> 10, of which waited for: 5 -> 5; matrix products, arithmetic and copies ran while one was open for 13% -> 23% of each run, Pallas kernels for 0% -> 0%
where the time goes in v1:
time: 1030 us; the launch traced here: 1020 us
  waiting for transfers between devices  481 us (47%)
  local copies, waits for them, and re-layouts  186 us (18%)
  blocking collectives  116 us (11%)
  matrix products  114 us (11%)
  other arithmetic  87.9 us (9%)
  starting transfers between devices  21.5 us (2%)
  between operations  15.7 us (2%)
    unnamed x7, waiting for transfers between devices  206 us
    psum x2, waiting for transfers between devices, per_device(): lax.psum((branch_part, depth_part, proj_part, class_part), 'rows')  172 us
    psum x1, blocking collectives, per_device(): pooled = lax.psum(column_sum, 'rows') / total_pixels  111 us
    psum x1, waiting for transfers between devices, per_device(): mixed = lax.psum(mixed_part, 'grp')  68.7 us
    dot_general x3, matrix products, per_device(): jnp.einsum('pd,cd->pc', grad_pre[k + 1], branch_weight[k + 1], preferred_...  68.6 us
    convert_element_type x3, other arithmetic, depth_taps(): outputs.append(total.astype(jnp.bfloat16))  67.9 us
    dynamic_update_slice x2, local copies, waits for them, and re-layouts, _supply_view(): lax.dynamic_update_slice_in_dim(frame_out, lower, (row_out - dev) % res *...  62.9 us
    dynamic_update_slice x1, local copies, waits for them, and re-layouts, _supply_view(): lax.dynamic_update_slice_in_dim(frame_out, kept_arr, (row_out + dev) % re...  34.9 us
  transfers between devices with their start and end apart: 10, of which 5 were waited for; matrix products, arithmetic and copies ran while one was open for 23% of the time, Pallas kernels for 0%

profile of v1, /device:TPU:0, one launch (start us, length us, event | category | flops | bytes accessed | tf_op | source)
XLA Modules:
  0.0 1022.8 jit_solution(9555941132302764137)
XLA Ops:
  7.2 5.2 fusion.69
  12.4 6.3 collective-permute-start
  18.7 1.3 collective-permute-start.1
  20.0 0.5 convert_reduce_fusion
  20.4 110.5 %psum.49 = f32[512]{0:T(512)S(1)} all-reduce(f32[512]{0:T(512)S(1)} %convert_reduce_fusion), channel_id=1, replica_groups=mesh['rows'=8,'grp'=4] {'rows'}, use_global_device_ids=true, to_apply=%region_2.3 | all-reduce | flops 512 | bytes 4096 | tf_op jit(solution)/shard_map/psum | solution.py:88
  131.0 1.1 convolution_bitcast_fusion.6
  132.2 1.9 convolution_bitcast_fusion.5
  134.2 8.2 maximum_convert_fusion
  142.4 24.1 %add_convert_fusion.1 = bf16[24,128,512]{2,1,0:T(8,128)(2,1)S(1)} fusion(f32[60,128,512]{2,1,0:T(8,128)} %maximum_convert_fusion, f32[512]{0:T(512)S(1)} %bitcast.246, f32[512]{0:T(512)S(1)} %bitcast.247, f32[512]{0:T(512)S(1)} %bitcast.248, f32[512]{0:T(512)S(1)} %bitcast.249, f32[512]{0:T(512)S(1)} %bitcast.250, f32[512]{0:T(512)S(1)} %bitcast.251, ...), kind=kLoop, calls=%fused_computation.49 | loop fusion | flops 28311552 | bytes 37767168 | tf_op jit(solution)/shard_map/convert_element_type | solution.py:37
  166.5 3.8 convolution_bitcast_fusion.3
  170.2 19.2 %add_convert_fusion = bf16[24,128,512]{2,1,0:T(8,128)(2,1)S(1)} fusion(f32[60,128,512]{2,1,0:T(8,128)} %maximum_convert_fusion, f32[512]{0:T(512)S(1)} %bitcast.234, f32[512]{0:T(512)S(1)} %bitcast.235, f32[512]{0:T(512)S(1)} %bitcast.239, f32[512]{0:T(512)S(1)} %bitcast.240, f32[512]{0:T(512)S(1)} %bitcast.241, f32[512]{0:T(512)S(1)} %bitcast.242, ...), kind=kLoop, calls=%fused_computation.48 | loop fusion | flops 28311552 | bytes 37767168 | tf_op jit(solution)/shard_map/convert_element_type | solution.py:37
  189.5 3.8 convolution_bitcast_fusion.2
  193.3 24.6 %add_convert_fusion.2 = bf16[24,128,512]{2,1,0:T(8,128)(2,1)S(1)} fusion(f32[60,128,512]{2,1,0:T(8,128)} %maximum_convert_fusion, f32[512]{0:T(512)S(1)} %bitcast.237, f32[512]{0:T(512)S(1)} %bitcast.238, f32[512]{0:T(512)S(1)} %bitcast.229, f32[512]{0:T(512)S(1)} %bitcast.230, f32[512]{0:T(512)S(1)} %bitcast.231, f32[512]{0:T(512)S(1)} %bitcast.232, ...), kind=kLoop, calls=%fused_computation.50 | loop fusion | flops 28311552 | bytes 37767168 | tf_op jit(solution)/shard_map/convert_element_type | solution.py:37
  217.9 1.6 copy-done.8
  219.5 2.7 convolution_bitcast_fusion.4
  222.3 4.8 pad_maximum_fusion
  227.1 15.3 %copy.19 = f32[4,3072,256]{1,0,2:T(4,128)} copy(f32[4,3072,256]{2,1,0:T(8,128)} %pad_maximum_fusion) | data formatting | bytes 25165824 | tf_op jit(solution)/shard_map/stack | solution.py:89
  242.5 12.1 %all-reduce.10.cloned.1.call-start = ((), (), s32[]{:S(2)}) async-start(), calls=%async_computation.1 | async-start | bytes 6291456 | tf_op jit(solution)/shard_map/psum | solution.py:105
  254.6 0.7 fusion.72
  255.9 0.8 copy.38
  256.8 0.1 fusion.50
  256.9 205.5 %all-reduce.12.cloned.1.call-done = f32[4,3072,256]{1,0,2:T(4,128)} async-done(((f32[4,3072,256]{1,0,2:T(4,128)}), f32[4,3072,256]{1,0,2:T(4,128)}) %all-reduce.12.cloned.1.call-update) | async-done | bytes 12582928
  462.4 2.1 constant_dynamic-slice_fusion
  464.5 1.6 copy-done.11
  466.2 3.8 fusion.1
  470.0 68.7 %all-reduce.10.cloned.1.call-done = f32[3072,256]{1,0:T(8,128)} async-done(((f32[3072,256]{1,0:T(8,128)}), f32[3072,256]{1,0:T(8,128)}) %all-reduce.10.cloned.1.call-update) | async-done | bytes 3145744 | tf_op jit(solution)/shard_map/psum | solution.py:105
  538.8 2.6 fusion.73
  541.4 3.2 convert_reduce_fusion.1
  544.6 4.5 fusion.3
  549.1 1.7 collective-permute-start.3
  550.8 34.6 %collective-permute-done.2 = bf16[4,3072,64]{1,2,0:T(8,128)(2,1)} collective-permute-done((bf16[4,3072,64]{1,2,0:T(8,128)(2,1)}, bf16[4,3072,64]{1,2,0:T(8,128)(2,1)}, u32[]{:S(2)}, u32[]{:S(2)}) %collective-permute-start.2) | collective-permute-done | bytes 1572896 | tf_op jit(solution)/shard_map/ppermute | solution.py:128
  585.4 4.1 copy.22
  589.5 3.0 broadcast_in_dim.6
  592.6 30.0 %dynamic_update_slice.12 = bf16[4,3072,256]{2,1,0:T(8,128)(2,1)} dynamic-update-slice(bf16[4,3072,256]{2,1,0:T(8,128)(2,1)} %broadcast_in_dim.6, bf16[4,3072,64]{2,1,0:T(8,128)(2,1)} %copy.22, s32[]{:T(128)} %constant.47.clone.1, s32[]{:T(128)} %constant.47.clone.1, s32[]{:T(128)S(6)} %select_n.27) | dynamic-update-slice | bytes 3145732 | tf_op jit(solution)/shard_map/dynamic_update_slice | solution.py:124
  622.5 2.8 fusion.26
  625.4 5.0 fusion.11
  630.4 4.2 copy.23
  634.5 34.0 %dynamic_update_slice.13 = bf16[4,3072,256]{2,1,0:T(8,128)(2,1)} dynamic-update-slice(bf16[4,3072,256]{2,1,0:T(8,128)(2,1)} %dynamic_update_slice.12, bf16[4,3072,64]{2,1,0:T(8,128)(2,1)} %copy.23, s32[]{:T(128)} %constant.47.clone.1, s32[]{:T(128)} %constant.47.clone.1, s32[]{:T(128)S(6)} %select_n.29) | dynamic-update-slice | bytes 3145732 | tf_op jit(solution)/shard_map/dynamic_update_slice | solution.py:129
  668.5 4.2 copy.24
  672.7 34.9 %dynamic_update_slice.14 = bf16[4,3072,256]{2,1,0:T(8,128)(2,1)} dynamic-update-slice(bf16[4,3072,256]{2,1,0:T(8,128)(2,1)} %dynamic_update_slice.13, bf16[4,3072,64]{2,1,0:T(8,128)(2,1)} %copy.24, s32[]{:T(128)} %constant.47.clone.1, s32[]{:T(128)} %constant.47.clone.1, s32[]{:T(128)S(6)} %select_n.31) | dynamic-update-slice | bytes 3145732 | tf_op jit(solution)/shard_map/dynamic_update_slice | solution.py:134
  707.6 4.2 copy.25
  711.8 28.9 %dynamic_update_slice.15 = bf16[4,3072,256]{2,1,0:T(8,128)(2,1)} dynamic-update-slice(bf16[4,3072,256]{2,1,0:T(8,128)(2,1)} %dynamic_update_slice.14, bf16[4,3072,64]{2,1,0:T(8,128)(2,1)} %copy.25, s32[]{:T(128)} %constant.47.clone.1, s32[]{:T(128)} %constant.47.clone.1, s32[]{:T(128)S(6)} %select_n.33) | dynamic-update-slice | bytes 3145732 | tf_op jit(solution)/shard_map/dynamic_update_slice | solution.py:129
  740.7 4.5 fusion.68
  745.2 0.7 copy-done.3
  745.9 3.8 fusion.14
  749.8 1.8 fusion.17
  751.6 1.8 fusion.20
  753.3 1.8 fusion.23
  755.1 24.8 %multiply_reduce_fusion.18 = (f32[512]{0:T(512)S(1)}, f32[512]{0:T(512)S(1)}, f32[512]{0:T(512)S(1)}, f32[512]{0:T(512)S(1)}, f32[512]{0:T(512)S(1)}, /*index=5*...) fusion(f32[60,128,512]{2,1,0:T(8,128)} %maximum_convert_fusion, ...), kind=kOutput, calls=%fused_computation.38 | convolution fusion | flops 833613312 | bytes 36456448 | tf_op jit(solution)/shard_map/pd,cd->pc/dot_general | solution.py:153
  780.0 24.3 %multiply_reduce_fusion.9 = (f32[512]{0:T(512)S(1)}, f32[512]{0:T(512)S(1)}, f32[512]{0:T(512)S(1)}, f32[512]{0:T(512)S(1)}, f32[512]{0:T(512)S(1)}, /*index=5*/...) fusion(f32[60,128,512]{2,1,0:T(8,128)} %maximum_convert_fusion, ...), kind=kOutput, calls=%fused_computation.29 | convolution fusion | flops 833613312 | bytes 36456448 | tf_op jit(solution)/shard_map/pd,cd->pc/dot_general | solution.py:153
  804.4 19.6 %multiply_reduce_fusion = (f32[512]{0:T(512)S(1)}, f32[512]{0:T(512)S(1)}, f32[512]{0:T(512)S(1)}, f32[512]{0:T(512)S(1)}, f32[512]{0:T(512)S(1)}, /*index=5*/f3...) fusion(f32[60,128,512]{2,1,0:T(8,128)} %maximum_convert_fusion, ...), kind=kOutput, calls=%fused_computation.20 | convolution fusion | flops 833613312 | bytes 36456448 | tf_op jit(solution)/shard_map/pd,cd->pc/dot_general | solution.py:153
  824.1 0.7 pad_maximum_fusion.3
  824.8 2.5 pad_maximum_fusion.1
  828.0 67.9 %all-reduce.14.cloned.1.call-done = (f32[3,3,3,512]{3,2,1,0:T(4,128)}, f32[256]{0:T(256)}, f32[256,11]{0,1:T(8,128)}) async-done(((f32[3,3,3,512]{3,2,1,0:T(4,128)}, f32[256]{0:T(256)}, f32[256,11]{0,1:T(8,128)}), (f32[3,3,3,512]{3,2,1,0:T(4,128)}, f32[256]{0:T(256)}, f32[256,11]{0,1:T(8,128)})) %all-reduce.14.cloned.1.call-update) | async-done | bytes 67600 | tf_op jit(solution)/shard_map/psum | solution.py:160
  895.9 0.9 fusion.25
  896.8 0.3 dynamic-update-slice
  897.1 5.6 all-reduce.1
  902.7 0.7 broadcast_multiply_fusion.1
  903.5 0.9 broadcast_multiply_fusion
  904.4 104.3 %all-reduce.16.cloned.1.call-done = (f32[4,512,256]{1,2,0:T(8,128)}, f32[4,64,256]{2,1,0:T(8,128)}) async-done(((f32[4,512,256]{1,2,0:T(8,128)}, f32[4,64,256]{2,1,0:T(8,128)}), (f32[4,512,256]{1,2,0:T(8,128)}, f32[4,64,256]{2,1,0:T(8,128)})) %all-reduce.16.cloned.1.call-update) | async-done | bytes 2359312 | tf_op jit(solution)/shard_map/psum | solution.py:160
  1008.6 2.9 copy.33
  1011.5 1.7 pad_maximum_fusion.2
  1013.2 1.5 copy.56
  1014.8 1.3 copy.57
  (74 shorter events, 0.7 us)
Async XLA Ops:
  7.2 123.8 %copy-start = (bf16[512,256]{1,0:T(8,128)(2,1)S(1)}, bf16[512,256]{1,0:T(8,128)(2,1)}, u32[]{:S(2)}) copy-start(bf16[512,256]{1,0:T(8,128)(2,1)} %param.10) | copy-start | bytes 786436
  7.2 12.8 %copy-start.2 = (bf16[24,128,512]{2,1,0:T(8,128)(2,1)S(1)}, bf16[24,128,512]{2,1,0:T(8,128)(2,1)}, u32[]{:S(2)}) copy-start(bf16[24,128,512]{2,1,0:T(8,128)(2,1)} %param.7) | copy-start | bytes 9437188
  7.2 125.0 %copy-start.20 = (f32[3,3,3,512]{3,2,1,0:T(4,128)S(1)}, f32[3,3,3,512]{3,2,1,0:T(4,128)}, u32[]{:S(2)}) copy-start(f32[3,3,3,512]{3,2,1,0:T(4,128)} %param.8) | copy-start | bytes 165892
  7.2 248.7 %reduce-scatter.4.cloned.1.call-start = ((), (), s32[]{:S(2)}) async-start(), calls=%async_computation.2 | async-start | bytes 163840
  12.4 121.8 %collective-permute-start = (bf16[18,128,512]{2,1,0:T(8,128)(2,1)}, bf16[18,128,512]{2,1,0:T(8,128)(2,1)}, u32[]{:S(2)}, u32[]{:S(2)}) collective-permute-start(bf16[18,128,512]{2,1,0:T(8,128)(2,1)} %get-tuple-element.50), channel_id=1, source_target_pairs={{0,4},{4,8},{8,12},{12,16},{16,20},{20,24},{24,28},{1,5},{5,9},{9,... | collective-permute-start | bytes 7077896 | tf_op jit(solution)/shard_map/ppermute | solution.py:16
  18.7 115.5 %collective-permute-start.1 = (bf16[18,128,512]{2,1,0:T(8,128)(2,1)}, bf16[18,128,512]{2,1,0:T(8,128)(2,1)}, u32[]{:S(2)}, u32[]{:S(2)}) collective-permute-start(bf16[18,128,512]{2,1,0:T(8,128)(2,1)} %get-tuple-element.51), channel_id=1, source_target_pairs={{4,0},{8,4},{12,8},{16,12},{20,16},{24,20},{28,24},{5,1},{9,5},{13... | collective-permute-start | bytes 7077896 | tf_op jit(solution)/shard_map/ppermute | solution.py:19
  132.1 330.3 %all-reduce.12.cloned.1.call-start = ((), (), s32[]{:S(2)}) async-start(), calls=%async_computation.3 | async-start | bytes 25165824
  166.4 23.0 %copy-start.4 = (bf16[24,128,512]{2,1,0:T(8,128)(2,1)}, bf16[24,128,512]{2,1,0:T(8,128)(2,1)S(1)}, u32[]{:S(2)}) copy-start(bf16[24,128,512]{2,1,0:T(8,128)(2,1)S(1)} %add_convert_fusion.1) | copy-start | bytes 9437188
  189.5 28.4 %copy-start.6 = (bf16[24,128,512]{2,1,0:T(8,128)(2,1)}, bf16[24,128,512]{2,1,0:T(8,128)(2,1)S(1)}, u32[]{:S(2)}) copy-start(bf16[24,128,512]{2,1,0:T(8,128)(2,1)S(1)} %add_convert_fusion) | copy-start | bytes 9437188
  217.9 1.6 copy-start.8
  217.9 4.3 copy-start.9
  217.9 4.3 copy-start.10
  242.4 12.1 %copy-start.23 = (u32[32]{0:T(128)S(1)}, u32[32]{0:T(128)}, u32[]{:S(2)}) copy-start(u32[32]{0:T(128)} %constant.60) | copy-start | bytes 388
  242.4 14.3 %copy-start.22 = (bf16[5,64,256]{2,1,0:T(8,128)(2,1)S(1)}, bf16[5,64,256]{2,1,0:T(8,128)(2,1)}, u32[]{:S(2)}) copy-start(bf16[5,64,256]{2,1,0:T(8,128)(2,1)} %param.11) | copy-start | bytes 491524
  242.5 296.3 %all-reduce.10.cloned.1.call-start = ((), (), s32[]{:S(2)}) async-start(), calls=%async_computation.1 | async-start | bytes 6291456 | tf_op jit(solution)/shard_map/psum | solution.py:105
  464.5 1.7 copy-start.11
  464.5 5.5 copy-start.19
  464.5 74.3 %copy-start.21 = (bf16[256,11]{0,1:T(8,128)(2,1)S(1)}, bf16[256,11]{0,1:T(8,128)(2,1)}, u32[]{:S(2)}) copy-start(bf16[256,11]{0,1:T(8,128)(2,1)} %param.12) | copy-start | bytes 16900
  470.0 426.0 %all-reduce.14.cloned.1.call-start = ((), (), s32[]{:S(2)}) async-start(), calls=%async_computation.4 | async-start | bytes 182272 | tf_op jit(solution)/shard_map/psum | solution.py:160
  538.8 5.8 copy-start.12
  544.6 4.5 copy-start.15
  549.1 36.3 %collective-permute-start.2 = (bf16[4,3072,64]{1,2,0:T(8,128)(2,1)}, bf16[4,3072,64]{1,2,0:T(8,128)(2,1)}, u32[]{:S(2)}, u32[]{:S(2)}) collective-permute-start(bf16[4,3072,64]{1,2,0:T(8,128)(2,1)} %fusion.3), channel_id=1, source_target_pairs={{0,1},{1,2},{2,3},{3,0},{4,5},{5,6},{6,7},{7,4},{8,9},{9,10},{10,1... | collective-permute-start | bytes 4718600 | tf_op jit(solution)/shard_map/ppermute | solution.py:128
  549.1 119.5 %collective-permute-start.3 = (bf16[4,3072,64]{1,2,0:T(8,128)(2,1)}, bf16[4,3072,64]{1,2,0:T(8,128)(2,1)}, u32[]{:S(2)}, u32[]{:S(2)}) collective-permute-start(bf16[4,3072,64]{1,2,0:T(8,128)(2,1)} %fusion.3), channel_id=1, source_target_pairs={{0,3},{1,0},{2,1},{3,2},{4,7},{5,4},{6,5},{7,6},{8,11},{9,8},{10,9... | collective-permute-start | bytes 4718600 | tf_op jit(solution)/shard_map/ppermute | solution.py:133
  585.4 122.2 %collective-permute-start.4 = (bf16[4,3072,64]{1,2,0:T(8,128)(2,1)}, bf16[4,3072,64]{1,2,0:T(8,128)(2,1)}, u32[]{:S(2)}, u32[]{:S(2)}) collective-permute-start(bf16[4,3072,64]{1,2,0:T(8,128)(2,1)} %collective-permute-done.2), channel_id=1, source_target_pairs={{0,1},{1,2},{2,3},{3,0},{4,5},{5,6},{6,7},{7,4},{8,9},{9,10},{10,1... | collective-permute-start | bytes 4718600 | tf_op jit(solution)/shard_map/ppermute | solution.py:128
  740.7 5.2 copy-start.3
  740.7 9.0 copy-start.5
  745.9 5.6 copy-start.7
  755.1 24.9 %copy-start.14 = (bf16[1,3072,256]{2,1,0:T(8,128)(2,1)S(1)}, bf16[1,3072,256]{2,1,0:T(8,128)(2,1)}, u32[]{:S(2)}) copy-start(bf16[1,3072,256]{2,1,0:T(8,128)(2,1)} %get-tuple-element.49) | copy-start | bytes 4718596
  780.0 24.4 %copy-start.13 = (bf16[1,3072,256]{2,1,0:T(8,128)(2,1)S(1)}, bf16[1,3072,256]{2,1,0:T(8,128)(2,1)}, u32[]{:S(2)}) copy-start(bf16[1,3072,256]{2,1,0:T(8,128)(2,1)} %get-tuple-element.48) | copy-start | bytes 4718596
  804.4 20.4 %copy-start.16 = (f32[1,512,256]{1,2,0:T(8,128)S(1)}, f32[1,512,256]{1,2,0:T(8,128)}, u32[]{:S(2)}) copy-start(f32[1,512,256]{1,2,0:T(8,128)} %fusion.14) | copy-start | bytes 1572868
  804.4 20.4 %copy-start.17 = (f32[1,512,256]{1,2,0:T(8,128)S(1)}, f32[1,512,256]{1,2,0:T(8,128)}, u32[]{:S(2)}) copy-start(f32[1,512,256]{1,2,0:T(8,128)} %fusion.17) | copy-start | bytes 1572868
  804.4 20.4 %copy-start.18 = (f32[1,512,256]{1,2,0:T(8,128)S(1)}, f32[1,512,256]{1,2,0:T(8,128)}, u32[]{:S(2)}) copy-start(f32[1,512,256]{1,2,0:T(8,128)} %fusion.20) | copy-start | bytes 1572868
  824.0 192.1 %copy-start.1 = (bf16[512,256]{1,0:T(8,128)(2,1)S(1)}, bf16[512,256]{1,0:T(8,128)(2,1)}, u32[]{:S(2)}) copy-start(bf16[512,256]{1,0:T(8,128)(2,1)} %param.10) | copy-start | bytes 786436
  824.7 183.9 %all-reduce.16.cloned.1.call-start = ((), (), s32[]{:S(2)}) async-start(), calls=%async_computation.5 | async-start | bytes 4718592 | tf_op jit(solution)/shard_map/psum | solution.py:160
Sparse Core Ops, SparseCore 0:
  132.2 18.7 reduce-scatter.3
  242.6 219.7 all-reduce.11
  470.1 68.6 all-reduce.9
  824.9 71.0 all-reduce.13
  900.4 108.2 all-reduce.15
